TPU v7x, 256 devices: a whole 4x4x8 slice. The times are simulated.
256 devices in a mesh: blk: 64 (over y, z, x_lo), vocab: 4 (over x_hi, core).
Axes of the slice: x: 4 (x_hi: 2, x_lo: 2; x = x_hi * 2 + x_lo), y: 4, z: 8, core: 2. Of those that a mesh axis runs over, the one named last changes fastest.
Arguments:
- hidden: bfloat16 [45056, 2304], P('blk'), may hold values from -6 to 6
- table: bfloat16 [131072, 2304], P(('blk', 'vocab')), may hold values from -0.25 to 0.25
- targets: int32 [45056], P('blk'), may hold values from 0 to 131071
- group_start: int32 [64], P('blk'), may hold values from 0 to 129024, as said below
- log_norm: float32 [45056], P('blk')
- loss_grad: float32 [45056], P('blk'), may hold values from 4 to 32
Outputs:
- grad_hidden: bfloat16 [45056, 2304], P(('blk', 'vocab'))
- grad_table: float32 [131072, 2304], P(('blk', 'vocab'))
Inputs may be any that keep to these rules, and one draw needn't show every extreme that they name: `group_start`: a permutation of the multiples of 2048 below 131072.
All inputs are finite; a program needn't handle non-finite values.
Results may differ from a plain program's by a relative error of at most 0.014.
Values may be sent and summed in bfloat16 or wider, within the bound.
A program may use at most 128 MiB of HBM per device.

v0:
```python
import jax
import jax.numpy as jnp
from jax import lax
from jax.sharding import PartitionSpec as P

ROUNDS = 3


def from_behind(value, axis, steps):
    count = lax.axis_size(axis)
    pairs = [(source, (source + steps) % count) for source in range(count)]
    return lax.ppermute(value, axis, pairs)


def per_device(hidden, table, targets, group_start, log_norm, loss_grad):
    part = lax.axis_index("vocab")
    rows = table.shape[0]
    ids_local = jnp.arange(rows, dtype=jnp.int32)
    hidden_acc = jnp.zeros(hidden.shape, jnp.float32)
    table_acc = jnp.zeros(table.shape, jnp.float32)
    piece = table
    first_id = group_start
    for r in range(ROUNDS):
        if r > 0:
            piece, first_id = from_behind((piece, first_id), "blk", 1)
        base = first_id[0] + part * rows
        logits = lax.dot_general(
            hidden, piece, (((1,), (1,)), ((), ())), preferred_element_type=jnp.float32
        )
        hit = (targets[:, None] == (base + ids_local)[None, :]).astype(jnp.float32)
        prob = jnp.exp(logits - log_norm[:, None])
        slope = (loss_grad[:, None] * (prob - hit)).astype(jnp.bfloat16)
        hidden_acc = hidden_acc + jnp.dot(slope, piece, preferred_element_type=jnp.float32)
        term = lax.dot_general(
            slope, hidden, (((0,), (0,)), ((), ())), preferred_element_type=jnp.float32
        )
        table_acc = table_acc + term
        if r < ROUNDS - 1:
            table_acc = from_behind(table_acc.astype(jnp.bfloat16), "blk", 1).astype(
                table_acc.dtype
            )
    grad_hidden = lax.psum_scatter(
        hidden_acc.astype(jnp.bfloat16), "vocab", scatter_dimension=0, tiled=True
    )
    return (grad_hidden, table_acc)


def solution(mesh):
    placed = (P("blk", None), P(("blk", "vocab"), None), P("blk"), P("blk"), P("blk"), P("blk"))
    return jax.shard_map(
        per_device,
        mesh=mesh,
        in_specs=placed,
        out_specs=(P(("blk", "vocab"), None), P(("blk", "vocab"), None)),
        check_vma=False,
    )
```

profile of v0, /device:TPU:1, one launch (start us, length us, event | category | flops | bytes accessed | tf_op | source)
XLA Modules:
  0.0 281.6 jit_solution(3353558658497451712)
XLA Ops:
  7.2 0.0 copy-start
  7.2 0.0 reduce-scatter.2.cloned.1.call-start
  7.2 2.1 collective-permute-start
  9.3 1.6 collective-permute-start.1
  11.6 56.7 %collective-permute-done = bf16[512,2304]{1,0:T(8,128)(2,1)} collective-permute-done((bf16[512,2304]{1,0:T(8,128)(2,1)}, bf16[512,2304]{1,0:T(8,128)(2,1)}, u32[]{:S(2)}, u32[]{:S(2)}) %collective-permute-start) | collective-permute-done | bytes 2359328 | tf_op jit(solution)/shard_map/ppermute | solution.py:12
  68.4 0.0 collective-permute-start.2
  68.4 0.0 copy-done
  68.4 0.0 copy-start.4
  68.4 0.0 copy-start.5
  68.4 0.0 copy-start.6
  68.4 0.0 copy-start.7
  68.4 3.7 %fusion.34 = f32[704,512]{1,0:T(8,128)S(1)} fusion(bf16[704,2304]{1,0:T(8,128)(2,1)S(1)} %copy-done, bf16[512,2304]{1,0:T(8,128)(2,1)} %param.7), kind=kOutput, calls=%fused_computation.44 | convolution fusion | flops 1660944384 | bytes 7045120 | tf_op jit(solution)/shard_map/dot_general | solution.py:27
  72.1 0.0 copy-done.4
  72.1 0.0 copy-done.5
  72.1 0.0 copy-done.6
  72.1 0.0 copy-done.7
  72.2 0.0 copy-start.3
  72.2 4.8 %fusion.7 = f32[704,2304]{1,0:T(8,128)} fusion(bf16[512,2304]{1,0:T(8,128)(2,1)S(1)} %copy-done.7, f32[704,512]{1,0:T(8,128)S(1)} %fusion.34, s32[512]{0:T(512)S(1)} %iota_add_fusion.2, f32[704]{0:T(1024)S(1)} %copy-done.4, f32[704]{0:T(1024)S(1)} %copy-done.5, s32[704]{0:T(1024)S(1)} %copy-done.6), kind=kOutput, calls=%fused_computation.14 | convolution fusion | flops 1663107072 | bytes 10299648 | tf_op jit(solution)/shard_map/dot_general | solution.py:33
  76.9 0.0 copy-done.3
  76.9 0.0 collective-permute-done.1
  77.6 0.3 collective-permute-start.3
  77.9 46.5 %collective-permute-done.3 = s32[1]{0:T(128)} collective-permute-done((s32[1]{0:T(128)}, s32[1]{0:T(128)}, u32[]{:S(2)}, u32[]{:S(2)}) %collective-permute-start.3) | collective-permute-done | bytes 36 | tf_op jit(solution)/shard_map/ppermute | solution.py:12
  125.1 3.5 %fusion.35 = f32[704,512]{1,0:T(8,128)S(1)} fusion(bf16[704,2304]{1,0:T(8,128)(2,1)S(1)} %copy-done, bf16[512,2304]{1,0:T(8,128)(2,1)} %collective-permute-done), kind=kOutput, calls=%fused_computation.45 | convolution fusion | flops 1660944384 | bytes 7045120 | tf_op jit(solution)/shard_map/dot_general | solution.py:27
  128.6 0.0 copy-start.8
  128.6 1.1 copy-done.8
  129.8 0.0 slice-start
  129.8 3.9 %fusion.4 = f32[704,2304]{1,0:T(8,128)S(1)} fusion(bf16[512,2304]{1,0:T(8,128)(2,1)} %collective-permute-done, f32[704,512]{1,0:T(8,128)S(1)} %fusion.35, s32[512]{0:T(512)S(1)} %iota_add_fusion.1, f32[704]{0:T(1024)S(1)} %copy-done.4, f32[704]{0:T(1024)S(1)} %copy-done.5, s32[704]{0:T(1024)S(1)} %copy-done.6), kind=kOutput, calls=%fused_computation.10 | convolution fusion | flops 1663107072 | bytes 10299648 | tf_op jit(solution)/shard_map/dot_general | solution.py:33
  133.7 0.0 slice-start.1
  133.7 0.0 collective-permute-done.2
  133.7 3.7 %fusion.36 = f32[704,512]{1,0:T(8,128)S(1)} fusion(bf16[704,2304]{1,0:T(8,128)(2,1)S(1)} %copy-done, bf16[512,2304]{1,0:T(8,128)(2,1)} %collective-permute-done.2), kind=kOutput, calls=%fused_computation.46 | convolution fusion | flops 1660944384 | bytes 7045120 | tf_op jit(solution)/shard_map/dot_general | solution.py:27
  137.4 0.0 copy-start.1
  137.4 1.1 copy-done.1
  138.5 0.0 slice-done
  138.5 0.0 slice-done.1
  138.5 5.4 %add_convert_fusion = bf16[704,2304]{1,0:T(8,128)(2,1)} fusion(f32[704,2304]{1,0:T(8,128)S(1)} %bitcast.17, f32[704,2304]{1,0:T(8,128)S(1)} %fusion.4, bf16[512,2304]{1,0:T(8,128)(2,1)} %collective-permute-done.2, f32[704,512]{1,0:T(8,128)S(1)} %fusion.36, s32[512]{0:T(512)S(1)} %iota_add_fusion, f32[704]{0:T(1024)S(1)} %copy-done.4, f32[704]{0:T(1024)S(1)} %copy-done.5, ...), kind=kOutput, calls=%fused_computation | convolution fusion | flops 1667973120 | bytes 20031744 | tf_op jit(solution)/shard_map/dot_general | solution.py:33
  143.9 0.0 reduce-scatter.2.cloned.1.call-update
  143.9 0.0 copy-start.9
  143.9 3.7 %convolution_convert_fusion = bf16[512,2304]{1,0:T(8,128)(2,1)S(1)} fusion(bf16[704,2304]{1,0:T(8,128)(2,1)S(1)} %copy-done, f32[704,512]{1,0:T(8,128)} %copy-done.3, s32[512]{0:T(512)S(1)} %iota_add_fusion.2, f32[704]{0:T(1024)S(1)} %copy-done.4, f32[704]{0:T(1024)S(1)} %copy-done.5, s32[704]{0:T(1024)S(1)} %copy-done.6), kind=kOutput, calls=%fused_computation.3 | convolution fusion | flops 1664286720 | bytes 7055616 | tf_op jit(solution)/shard_map/dot_general | solution.py:34
  147.7 0.0 copy-start.2
  147.7 0.1 collective-permute-start.4
  147.8 66.0 %collective-permute-done.4 = bf16[512,2304]{1,0:T(8,128)(2,1)S(1)} collective-permute-done((bf16[512,2304]{1,0:T(8,128)(2,1)S(1)}, bf16[512,2304]{1,0:T(8,128)(2,1)S(1)}, u32[]{:S(2)}, u32[]{:S(2)}) %collective-permute-start.4) | collective-permute-done | bytes 2359328 | tf_op jit(solution)/shard_map/ppermute | solution.py:12
  213.7 0.0 copy-done.9
  213.7 2.3 add_convert_fusion.1
  216.0 2.4 collective-permute-start.5
  218.4 51.8 %collective-permute-done.5 = bf16[512,2304]{1,0:T(8,128)(2,1)S(1)} collective-permute-done((bf16[512,2304]{1,0:T(8,128)(2,1)S(1)}, bf16[512,2304]{1,0:T(8,128)(2,1)S(1)}, u32[]{:S(2)}, u32[]{:S(2)}) %collective-permute-start.5) | collective-permute-done | bytes 2359328 | tf_op jit(solution)/shard_map/ppermute | solution.py:12
  270.2 0.0 copy-done.2
  270.2 4.5 %convert_add_fusion = f32[512,2304]{1,0:T(8,128)} fusion(bf16[512,2304]{1,0:T(8,128)(2,1)S(1)} %collective-permute-done.5, bf16[704,2304]{1,0:T(8,128)(2,1)S(1)} %copy-done, f32[704,512]{1,0:T(8,128)S(1)} %copy-done.2, s32[512]{0:T(512)S(1)} %iota_add_fusion, f32[704]{0:T(1024)S(1)} %copy-done.4, f32[704]{0:T(1024)S(1)} %copy-done.5, s32[704]{0:T(1024)S(1)} %copy-done.6), kind=kOutput, calls=%fused_computation.1 | convolution fusion | flops 1665466368 | bytes 11774208 | tf_op jit(solution)/shard_map/dot_general | solution.py:34
  274.7 0.0 reduce-scatter.2.cloned.1.call-done
  (4 shorter events, 0.0 us)
Async XLA Ops:
  7.2 61.2 %copy-start = (bf16[704,2304]{1,0:T(8,128)(2,1)S(1)}, bf16[704,2304]{1,0:T(8,128)(2,1)}, u32[]{:S(2)}) copy-start(bf16[704,2304]{1,0:T(8,128)(2,1)} %param.6) | copy-start | bytes 9732100
  7.2 267.5 %reduce-scatter.2.cloned.1.call-start = ((), (), s32[]{:S(2)}) async-start(), calls=%async_computation.1 | async-start | bytes 4055040 | tf_op jit(solution)/shard_map/reduce_scatter | solution.py:42
  7.2 61.2 %collective-permute-start = (bf16[512,2304]{1,0:T(8,128)(2,1)}, bf16[512,2304]{1,0:T(8,128)(2,1)}, u32[]{:S(2)}, u32[]{:S(2)}) collective-permute-start(bf16[512,2304]{1,0:T(8,128)(2,1)} %param.7), channel_id=1, source_target_pairs={{0,4},{4,8},{8,12},{12,16},{16,20},{20,24},{24,28},{28,32},{32,36}... | collective-permute-start | bytes 7077896 | tf_op jit(solution)/shard_map/ppermute | solution.py:12
  9.3 67.6 %collective-permute-start.1 = (s32[1]{0:T(128)}, s32[1]{0:T(128)}, u32[]{:S(2)}, u32[]{:S(2)}) collective-permute-start(s32[1]{0:T(128)} %param.9), channel_id=1, source_target_pairs={{0,4},{4,8},{8,12},{12,16},{16,20},{20,24},{24,28},{28,32},{32,36}... | collective-permute-start | bytes 20 | tf_op jit(solution)/shard_map/ppermute | solution.py:12
  68.4 65.3 %collective-permute-start.2 = (bf16[512,2304]{1,0:T(8,128)(2,1)}, bf16[512,2304]{1,0:T(8,128)(2,1)}, u32[]{:S(2)}, u32[]{:S(2)}) collective-permute-start(bf16[512,2304]{1,0:T(8,128)(2,1)} %collective-permute-done), channel_id=1, source_target_pairs={{0,4},{4,8},{8,12},{12,16},{16,20},{20,24},{24,28},{28,32},{32,36}... | collective-permute-start | bytes 7077896 | tf_op jit(solution)/shard_map/ppermute | solution.py:12
  68.4 3.7 %copy-start.4 = (f32[704]{0:T(1024)S(1)}, f32[704]{0:T(1024)}, u32[]{:S(2)}) copy-start(f32[704]{0:T(1024)} %param.10) | copy-start | bytes 8452
  68.4 3.7 %copy-start.5 = (f32[704]{0:T(1024)S(1)}, f32[704]{0:T(1024)}, u32[]{:S(2)}) copy-start(f32[704]{0:T(1024)} %param.11) | copy-start | bytes 8452
  68.4 3.7 %copy-start.6 = (s32[704]{0:T(1024)S(1)}, s32[704]{0:T(1024)}, u32[]{:S(2)}) copy-start(s32[704]{0:T(1024)} %param.8) | copy-start | bytes 8452
  68.4 3.7 %copy-start.7 = (bf16[512,2304]{1,0:T(8,128)(2,1)S(1)}, bf16[512,2304]{1,0:T(8,128)(2,1)}, u32[]{:S(2)}) copy-start(bf16[512,2304]{1,0:T(8,128)(2,1)} %param.7) | copy-start | bytes 7077892
  72.2 4.8 %copy-start.3 = (f32[704,512]{1,0:T(8,128)}, f32[704,512]{1,0:T(8,128)S(1)}, u32[]{:S(2)}) copy-start(f32[704,512]{1,0:T(8,128)S(1)} %fusion.34) | copy-start | bytes 4325380
  77.6 46.8 %collective-permute-start.3 = (s32[1]{0:T(128)}, s32[1]{0:T(128)}, u32[]{:S(2)}, u32[]{:S(2)}) collective-permute-start(s32[1]{0:T(128)} %collective-permute-done.1), channel_id=1, source_target_pairs={{0,4},{4,8},{8,12},{12,16},{16,20},{20,24},{24,28},{28,32},{32,36}... | collective-permute-start | bytes 20 | tf_op jit(solution)/shard_map/ppermute | solution.py:12
  128.6 1.1 copy-start.8
  129.8 8.7 %slice-start = ((s8[6488064]{0:T(1024)(128)(4,1)}), s8[4194304]{0:T(1024)(128)(4,1)S(1)}, s32[]{:S(2)}) async-start(s8[6488064]{0:T(1024)(128)(4,1)} %bitcast.16), calls=%async_computation.2 | async-start | bytes 8388608
  133.7 4.8 %slice-start.1 = ((s8[6488064]{0:T(1024)(128)(4,1)}), s8[2293760]{0:T(1024)(128)(4,1)S(1)}, s32[]{:S(2)}) async-start(s8[6488064]{0:T(1024)(128)(4,1)} %bitcast.16), calls=%async_computation.3 | async-start | bytes 4587520
  137.4 1.1 copy-start.1
  143.9 69.8 %copy-start.9 = (f32[704,512]{1,0:T(8,128)S(1)}, f32[704,512]{1,0:T(8,128)}, u32[]{:S(2)}) copy-start(f32[704,512]{1,0:T(8,128)} %copy-done.8) | copy-start | bytes 4325380
  147.7 122.6 %copy-start.2 = (f32[704,512]{1,0:T(8,128)S(1)}, f32[704,512]{1,0:T(8,128)}, u32[]{:S(2)}) copy-start(f32[704,512]{1,0:T(8,128)} %copy-done.1) | copy-start | bytes 4325380
  147.7 66.1 %collective-permute-start.4 = (bf16[512,2304]{1,0:T(8,128)(2,1)S(1)}, bf16[512,2304]{1,0:T(8,128)(2,1)S(1)}, u32[]{:S(2)}, u32[]{:S(2)}) collective-permute-start(bf16[512,2304]{1,0:T(8,128)(2,1)S(1)} %convolution_convert_fusion), channel_id=1, source_target_pairs={{0,4},{4,8},{8,12},{12,16},{16,20},{20,24},{24,28},{28,32},{32,36}... | collective-permute-start | bytes 7077896 | tf_op jit(solution)/shard_map/ppermute | solution.py:12
  216.0 54.2 %collective-permute-start.5 = (bf16[512,2304]{1,0:T(8,128)(2,1)S(1)}, bf16[512,2304]{1,0:T(8,128)(2,1)S(1)}, u32[]{:S(2)}, u32[]{:S(2)}) collective-permute-start(bf16[512,2304]{1,0:T(8,128)(2,1)S(1)} %add_convert_fusion.1), channel_id=1, source_target_pairs={{0,4},{4,8},{8,12},{12,16},{16,20},{20,24},{24,28},{28,32},{32,36}... | collective-permute-start | bytes 7077896 | tf_op jit(solution)/shard_map/ppermute | solution.py:12
Sparse Core Ops, SparseCore 0:
  144.0 64.9 reduce-scatter.1
where the time goes:
time: 284 us; the launch traced here: 282 us
  waiting for transfers between devices  221 us (78%)
  matrix products  35.5 us (12%)
  between operations  16.2 us (6%)
  starting transfers between devices  6.5 us (2%)
    ppermute x6, waiting for transfers between devices, from_behind(): return lax.ppermute(value, axis, pairs)  221 us
    dot_general x3, matrix products, per_device(): jnp.dot(slope, piece, preferred_element_type=jnp.float32)  14.1 us
    dot_general x3, matrix products, per_device(): lax.dot_general(hidden, piece, (((1,), (1,)), ((), ())), preferred_elemen...  10.9 us
    dot_general x3, matrix products, per_device(): lax.dot_general(slope, hidden, (((0,), (0,)), ((), ())), preferred_elemen...  10.5 us
    ppermute x6, starting transfers between devices, from_behind(): return lax.ppermute(value, axis, pairs)  6.46 us
  transfers between devices with their start and end apart: 7, of which 4 were waited for; matrix products, arithmetic and copies ran while one was open for 9% of the time, Pallas kernels for 0%

commit v1 on v0

v1 whole, which is shorter than its diff:
```python
import functools

import jax
import jax.numpy as jnp
from jax import lax
from jax.experimental import pallas as pl
from jax.experimental.pallas import tpu as pltpu
from jax.sharding import PartitionSpec as P

MESH = pl.DeviceIdType.MESH
CHUNKS = 4
GROUP = 256
WIDE = 768
F32, BF16 = jnp.float32, jnp.bfloat16


def remote(src, dst, sems, device):
    return pltpu.make_async_remote_copy(
        src_ref=src, dst_ref=dst, send_sem=sems[0], recv_sem=sems[1],
        device_id=device, device_id_type=MESH,
    )


def kernel(
    rows_of_ring, aux_ref, hid_hbm, tab_hbm, gh_out, gt_out,
    hid, oth, tab, arr, aux_oth, aux_arr, cols,
    s_own, s_oth, s_arr, t_own, t_oth, t_arr,
    grad, dwp, dwr, keep, cc_out, cc_in, x_out, x_in, gh_vmem,
    lsem, osem, bs, br, ts, tr, ps, pr, hs, hr, rs, rr, cs, cr, xs, xr, as_, ar,
):
    tokens, width = hid.shape
    vocab = tab.shape[0]
    quarter = tokens // 4
    blk, part = lax.axis_index("blk"), lax.axis_index("vocab")
    row, lo = blk // 2, blk % 2
    hi, core = part // 2, part % 2

    def at(r, low, high, c):
        return (((r + rows_of_ring) % rows_of_ring) * 2 + low, high * 2 + c)

    up, down = at(row + 1, lo, hi, core), at(row - 1, lo, hi, core)
    across = at(row, lo, 1 - hi, core)
    side = [at(row, 1 - lo, h, core) for h in range(2)]
    sibling = at(row, lo, hi, 1 - core)

    load_hid = pltpu.make_async_copy(hid_hbm, hid, lsem.at[0])
    load_tab = pltpu.make_async_copy(tab_hbm, tab, lsem.at[1])
    load_hid.start()
    load_tab.start()

    barrier = pltpu.get_barrier_semaphore()
    for device in (up, down, across, side[0], side[1], sibling):
        pl.semaphore_signal(barrier, inc=1, device_id=device, device_id_type=MESH)
    pl.semaphore_wait(barrier, 6)

    def quarter_of(h, c):
        return pl.ds(pl.multiple_of((h * 2 + c) * quarter, 16), quarter)

    aux_side = remote(aux_ref, aux_oth, (as_.at[0], ar.at[0]), at(row, 1 - lo, hi, core))
    aux_up = remote(aux_ref, aux_arr, (as_.at[1], ar.at[1]), up)
    aux_side.start()
    aux_up.start()

    piece = vocab // CHUNKS

    def piece_of(i):
        return pl.ds(i * piece, piece)

    table_up = [
        remote(tab_hbm.at[piece_of(i)], arr.at[piece_of(i)], (ts.at[i], tr.at[i]), up)
        for i in range(CHUNKS)
    ]
    grad_up = [
        remote(dwp.at[piece_of(i)], dwr.at[piece_of(i)], (ps.at[i], pr.at[i]), up)
        for i in range(CHUNKS)
    ]
    table_up[0].start()
    table_up[1].start()

    mine = quarter_of(hi, core)
    hidden_out = [
        remote(hid_hbm.at[mine], oth.at[mine], (hs.at[h], hr.at[hi]), side[h]) for h in range(2)
    ]
    hidden_in = [
        remote(oth.at[quarter_of(h, core)], oth.at[quarter_of(h, core)], (hs.at[h], hr.at[h]), side[h])
        for h in range(2)
    ]
    for copy in hidden_out:
        copy.start()

    def spread(ref, slot):
        for i in range(ref.shape[1] // 128):
            block = ref[:, i * 128:(i + 1) * 128]
            square = jnp.concatenate([block] * 16, axis=0)
            height = min(128, tokens - i * 128)
            cols[slot, i * 128:i * 128 + height, :] = square.T[:height]

    def slope(hid_ref, tab_ref, slot, base, out, out_t, start):
        group = pl.ds(start, GROUP)
        logits = lax.dot_general(
            hid_ref[...], tab_ref[group, :], (((1,), (1,)), ((), ())), preferred_element_type=F32
        )
        ids = (lax.broadcasted_iota(jnp.int32, (1, GROUP), 1) + (part * vocab + start)).astype(F32)
        hit = (cols[slot, :, 0:1] == base + ids).astype(F32)
        value = cols[slot, :, 2:3] * (jnp.exp(logits - cols[slot, :, 1:2]) - hit)
        out[:, group] = value.astype(BF16)
        out_t[group, :] = value.T.astype(BF16)

    def each_group(body):
        def step(i, carry):
            body(pl.multiple_of(i * GROUP, GROUP))
            return carry
        lax.fori_loop(0, vocab // GROUP, step, 0)

    def each_wide(body):
        def step(i, carry):
            body(pl.ds(pl.multiple_of(i * WIDE, WIDE), WIDE))
            return carry
        lax.fori_loop(0, width // WIDE, step, 0)

    def table_term(terms, start, out, dtype):
        group = pl.ds(start, GROUP)

        def body(wide):
            total = None
            for st, h in terms:
                term = jnp.dot(st[group, :], h[:, wide], preferred_element_type=F32)
                total = term if total is None else total + term
            out[group, wide] = total.astype(dtype)
        each_wide(body)

    def hidden_term(terms, rows, store):
        def body(wide):
            total = None
            for s, t in terms:
                term = jnp.dot(s[rows, :], t[:, wide], preferred_element_type=F32)
                total = term if total is None else total + term
            store(wide, total)
        each_wide(body)

    def core_copy(tok, h):
        slot = tok * 2 + h
        return remote(cc_out.at[slot], cc_in.at[slot], (cs.at[slot], cr.at[slot]), sibling)

    def halve(tok, terms):
        for h in range(2):
            def put(wide, value, slot=tok * 2 + h):
                cc_out[slot, :, wide] = value.astype(BF16)
            hidden_term(terms, quarter_of(h, 1 - core), put)
            core_copy(tok, h).start()
        for h in range(2):
            def put(wide, value, slot=tok * 2 + h):
                keep[slot, :, wide] = value
            hidden_term(terms, quarter_of(h, core), put)

    def x_copy(slot, dst_slot, device):
        return remote(x_out.at[slot], x_in.at[dst_slot], (xs.at[slot], xr.at[dst_slot]), device)

    def send_other():
        for h in range(2):
            core_copy(1, h).wait_recv()
            x_out[1 + h] = (keep[2 + h] + cc_in[2 + h].astype(F32)).astype(BF16)
            x_copy(1 + h, 1 + hi, side[h]).start()

    spread(aux_ref, 0)
    load_hid.wait()
    load_tab.wait()
    base_own = aux_ref[3:4, 0:1]
    each_group(lambda start: slope(hid, tab, 0, base_own, s_own, t_own, start))

    relay = [
        remote(oth.at[quarter_of(h, core)], oth.at[quarter_of(h, core)], (rs.at[h], rr.at[h]), sibling)
        for h in range(2)
    ]
    table_up[0].wait_send()
    table_up[2].start()
    for h in range(2):
        hidden_in[h].wait_recv()
        relay[h].start()
    aux_side.wait_recv()
    spread(aux_oth, 1)
    for h in range(2):
        relay[h].wait_recv()

    @pl.when(lo == 0)
    def _():
        each_group(lambda start: slope(oth, tab, 1, base_own, s_oth, t_oth, start))
        each_group(lambda start: table_term([(t_own, hid), (t_oth, oth)], start, dwp, BF16))
        halve(1, [(s_oth, tab)])
        send_other()

    @pl.when(lo == 1)
    def _():
        each_group(lambda start: table_term([(t_own, hid)], start, dwp, BF16))

    aux_up.wait_recv()
    base_arr = aux_arr[3:4, 0:1]
    table_up[1].wait_send()
    table_up[3].start()

    def arrived(start):
        slope(hid, arr, 0, base_arr, s_arr, t_arr, start)

        @pl.when(lo == 0)
        def _():
            table_term([(t_arr, hid)], start, grad, F32)

        @pl.when(lo == 1)
        def _():
            slope(oth, arr, 1, base_arr, s_oth, t_oth, start)
            table_term([(t_arr, hid), (t_oth, oth)], start, grad, F32)

    table_up[0].wait_recv()
    table_up[1].wait_recv()
    arrived(0)
    table_up[2].wait_send()
    grad_up[0].start()
    table_up[3].wait_send()
    grad_up[1].start()
    table_up[2].wait_recv()
    table_up[3].wait_recv()
    arrived(GROUP)

    @pl.when(lo == 1)
    def _():
        halve(1, [(s_oth, arr)])
        send_other()

    halve(0, [(s_own, tab), (s_arr, arr)])
    for h in range(2):
        core_copy(0, h).wait_recv()
    x_out[0] = (keep[1 - hi] + cc_in[1 - hi].astype(F32)).astype(BF16)
    x_copy(0, 0, across).start()
    grad_up[0].wait_send()
    grad_up[2].start()
    grad_up[1].wait_send()
    grad_up[3].start()

    outs = [
        pltpu.make_async_copy(grad.at[piece_of(i)], gt_out.at[piece_of(i)], osem.at[i])
        for i in range(CHUNKS)
    ]

    def finish(i):
        grad_up[i].wait_recv()
        grad[piece_of(i)] = grad[piece_of(i)] + dwr[piece_of(i)].astype(F32)
        outs[i].start()

    finish(0)
    finish(1)
    for slot, device in ((0, across), (1, side[0]), (2, side[1])):
        x_copy(slot, slot, device).wait_recv()
    total = keep[hi] + cc_in[hi].astype(F32)
    for slot in range(3):
        total = total + x_in[slot].astype(F32)
    gh_vmem[...] = total.astype(BF16)
    out_gh = pltpu.make_async_copy(gh_vmem, gh_out, osem.at[CHUNKS])
    out_gh.start()
    for i in range(2, CHUNKS):
        finish(i)

    aux_side.wait_send()
    aux_up.wait_send()
    for copy in hidden_out:
        copy.wait_send()
    for copy in relay:
        copy.wait_send()
    for tok in range(2):
        for h in range(2):
            core_copy(tok, h).wait_send()
    for slot, device in ((0, across), (1, side[0]), (2, side[1])):
        x_copy(slot, slot, device).wait_send()
    grad_up[2].wait_send()
    grad_up[3].wait_send()
    out_gh.wait()
    for copy in outs:
        copy.wait()


def per_device(rows_of_ring, hidden, table, targets, group_start, log_norm, loss_grad):
    tokens, width = hidden.shape
    vocab = table.shape[0]
    quarter = tokens // 4
    padded = -(-tokens // 128) * 128
    aux = jnp.stack([
        targets.astype(F32), log_norm, loss_grad,
        jnp.broadcast_to(group_start.astype(F32), (tokens,)),
    ])
    aux = jnp.pad(aux, ((0, 4), (0, padded - tokens)))
    dma = pltpu.SemaphoreType.DMA
    return pl.pallas_call(
        functools.partial(kernel, rows_of_ring),
        out_shape=(
            jax.ShapeDtypeStruct((quarter, width), BF16),
            jax.ShapeDtypeStruct((vocab, width), F32),
        ),
        in_specs=[
            pl.BlockSpec(memory_space=pltpu.VMEM),
            pl.BlockSpec(memory_space=pl.ANY),
            pl.BlockSpec(memory_space=pl.ANY),
        ],
        out_specs=[pl.BlockSpec(memory_space=pl.ANY)] * 2,
        scratch_shapes=[
            pltpu.VMEM((tokens, width), BF16),
            pltpu.VMEM((tokens, width), BF16),
            pltpu.VMEM((vocab, width), BF16),
            pltpu.VMEM((vocab, width), BF16),
            pltpu.VMEM((8, padded), F32),
            pltpu.VMEM((8, padded), F32),
            pltpu.VMEM((2, tokens, 128), F32),
            pltpu.VMEM((tokens, vocab), BF16),
            pltpu.VMEM((tokens, vocab), BF16),
            pltpu.VMEM((tokens, vocab), BF16),
            pltpu.VMEM((vocab, tokens), BF16),
            pltpu.VMEM((vocab, tokens), BF16),
            pltpu.VMEM((vocab, tokens), BF16),
            pltpu.VMEM((vocab, width), F32),
            pltpu.VMEM((vocab, width), BF16),
            pltpu.VMEM((vocab, width), BF16),
            pltpu.VMEM((4, quarter, width), F32),
            pltpu.VMEM((4, quarter, width), BF16),
            pltpu.VMEM((4, quarter, width), BF16),
            pltpu.VMEM((3, quarter, width), BF16),
            pltpu.VMEM((3, quarter, width), BF16),
            pltpu.VMEM((quarter, width), BF16),
            dma((2,)), dma((CHUNKS + 1,)),
            dma((1,)), dma((1,)),
            dma((CHUNKS,)), dma((CHUNKS,)),
            dma((CHUNKS,)), dma((CHUNKS,)),
            dma((2,)), dma((2,)),
            dma((2,)), dma((2,)),
            dma((4,)), dma((4,)),
            dma((3,)), dma((3,)),
            dma((2,)), dma((2,)),
        ],
        compiler_params=pltpu.CompilerParams(
            collective_id=1, has_side_effects=True, vmem_limit_bytes=60 * 2**20
        ),
        cost_estimate=pl.CostEstimate(
            flops=18 * tokens * vocab * width, bytes_accessed=12 * tokens * width, transcendentals=3 * tokens * vocab
        ),
    )(aux, hidden, table)


def solution(mesh):
    placed = (P("blk", None), P(("blk", "vocab"), None), P("blk"), P("blk"), P("blk"), P("blk"))
    return jax.shard_map(
        functools.partial(per_device, mesh.shape["blk"] // 2),
        mesh=mesh,
        in_specs=placed,
        out_specs=(P(("blk", "vocab"), None), P(("blk", "vocab"), None)),
        check_vma=False,
    )
```

time: 284 us -> 127 us (0.45)
  waiting for transfers between devices: 221 us -> 0 us
  Pallas kernels: 0 us -> 116 us
  matrix products: 35.5 us -> 0 us
  between operations: 16.2 us -> 1.29 us
  local copies, waits for them, and re-layouts: 2.28 us -> 8.98 us
  starting transfers between devices: 6.5 us -> 0 us
    ppermute x6 -> x0, waiting for transfers between devices: 221 us -> none  [from_behind(): return lax.ppermute(value, axis, pairs)]
    pallas_call x0 -> x1, Pallas kernels: none -> 116 us  [per_device(): pl.pallas_call(functools.partial(kernel, rows_of_ring), out_shape=(jax.Sh...]
    dot_general x9 -> x0, matrix products: 35.5 us -> none  [the longest x3 14.1 us: per_device(): jnp.dot(slope, piece, preferred_element_type=jnp.float32)]
    ppermute x6 -> x0, starting transfers between devices: 6.46 us -> none  [from_behind(): return lax.ppermute(value, axis, pairs)]
    unnamed x24 -> x2, local copies, waits for them, and re-layouts: 2.28 us -> 6.91 us
  transfers between devices with their start and end apart: 7 -> 0, of which waited for: 4 -> 0; matrix products, arithmetic and copies ran while one was open for 9% -> 0% of each run, Pallas kernels for 0% -> 0%
where the time goes in v1:
time: 127 us
  Pallas kernels  116 us (91%)
  local copies, waits for them, and re-layouts  8.98 us (7%)
  between operations  1.29 us (1%)
    pallas_call x1, Pallas kernels, per_device(): pl.pallas_call(functools.partial(kernel, rows_of_ring), out_shape=(jax.Sh...  116 us
    unnamed x2, local copies, waits for them, and re-layouts  6.91 us

profile of v1, /device:TPU:1, one launch (start us, length us, event | category | flops | bytes accessed | tf_op | source)
XLA Modules:
  0.0 126.7 jit_solution(3765081595946059772)
XLA Ops:
  1.3 0.1 pad.8.clone
  1.4 0.7 stack.13
  2.0 0.7 stack.14
  2.7 0.7 convert_element_type.10
  3.4 0.1 maximum_maximum_fusion
  3.5 0.6 pad.4.aux_ref
  4.1 115.6 %shard_map.77 = (bf16[176,2304]{1,0:T(8,128)(2,1)}, f32[512,2304]{1,0:T(8,128)}) custom-call(f32[8,768]{1,0:T(8,128)} %pad.4.aux_ref, bf16[704,2304]{1,0:T(8,128)(2,1)} %hid_hbm.1, bf16[512,2304]{1,0:T(8,128)(2,1)} %tab_hbm.1), custom_call_target="tpu_custom_call" | custom-call | flops 14948499456 | bytes 19464192 | tf_op jit(solution)/shard_map/pallas_call | solution.py:291
  119.8 2.1 %copy.11 = bf16[176,2304]{1,0:T(8,128)(2,1)} copy(bf16[176,2304]{1,0:T(8,128)(2,1)} %get-tuple-element.4) | data formatting | bytes 1622016
  121.8 4.8 %copy.12 = f32[512,2304]{1,0:T(8,128)} copy(f32[512,2304]{1,0:T(8,128)} %get-tuple-element.5) | data formatting | bytes 9437184
  (1 shorter events, 0.0 us)

commit v2 on v1

v2 whole, which is shorter than its diff:
```python
import functools

import jax
import jax.numpy as jnp
from jax import lax
from jax.experimental import pallas as pl
from jax.experimental.pallas import tpu as pltpu
from jax.sharding import PartitionSpec as P

MESH = pl.DeviceIdType.MESH
GROUP = 256
WIDE = 768
RING, LEG = 8, 3
TABLE_CUTS = tuple((64 * i, 64) for i in range(8))
GRAD_CUTS = tuple((64 * i, 64) for i in range(6)) + ((384, 48),)
LONG_FROM = 432
LONG_CUTS = ((432, 48), (480, 32))
F32, BF16 = jnp.float32, jnp.bfloat16

AUX, SIDE_HID, SIDE_RELAY, CORE, ACROSS = 0, 2, 4, 6, 10
TABLE = 13
GRAD = TABLE + len(TABLE_CUTS)
LONG = GRAD + len(GRAD_CUTS)
COPIES = LONG + 6


def kernel(
    rows_of_ring, tgt_ref, first_ref, norm_ref, cot_ref, hid_hbm, tab_hbm, gh_out, grad,
    hid, oth, tab, arr, aux_ref, aux_oth, aux_arr, cols,
    s_own, s_oth, s_arr, t_own, t_oth, t_arr,
    dwp, dwr, keep, give, cc_out, cc_in, x_out, x_in, way_a, way_b, lsem, send, recv,
):
    tokens, width = hid.shape
    vocab = tab.shape[0]
    quarter = tokens // 4
    blk, part = lax.axis_index("blk"), lax.axis_index("vocab")
    row, lo = blk // 2, blk % 2
    hi, core = part // 2, part % 2
    plane, height = row // RING, row % RING

    def at(r, low, high, c):
        return (((r + rows_of_ring) % rows_of_ring) * 2 + low, high * 2 + c)

    def along(y, z):
        return y * RING + (z + RING) % RING

    up, down = at(row + 1, lo, hi, core), at(row - 1, lo, hi, core)
    across = at(row, lo, 1 - hi, core)
    side = [at(row, 1 - lo, h, core) for h in range(2)]
    sibling = at(row, lo, hi, 1 - core)
    turn_to = lax.rem(height + RING + LEG, RING) == RING - 1
    turn_from = lax.rem(height + 2 * LEG, RING) == RING - 1
    leg_to = at(along(plane, height - LEG), lo, hi, core)
    leg_from = at(along(plane, height + LEG), lo, hi, core)
    turn_to = at(along(plane + turn_to.astype(jnp.int32), height - LEG), lo, hi, core)
    turn_from = at(along(plane - turn_from.astype(jnp.int32), height + LEG), lo, hi, core)
    last_to = at(along(plane, height - 1), lo, hi, core)
    last_from = at(along(plane, height + 1), lo, hi, core)

    load_hid = pltpu.make_async_copy(hid_hbm, hid, lsem.at[0])
    load_tab = pltpu.make_async_copy(tab_hbm, tab, lsem.at[1])
    load_hid.start()
    load_tab.start()

    aux_ref[...] = jnp.zeros_like(aux_ref)
    aux_ref[0:1, :tokens] = tgt_ref[...].astype(F32).reshape(1, tokens)
    aux_ref[1:2, :tokens] = norm_ref[...].reshape(1, tokens)
    aux_ref[2:3, :tokens] = cot_ref[...].reshape(1, tokens)
    aux_ref[3:4, :] = jnp.full((1, aux_ref.shape[1]), first_ref[0].astype(F32), F32)

    barrier = pltpu.get_barrier_semaphore()
    partners = (up, down, across, side[0], side[1], sibling, leg_to, leg_from, turn_to, turn_from, last_to, last_from)
    for device in partners:
        pl.semaphore_signal(barrier, inc=1, device_id=device, device_id_type=MESH)
    pl.semaphore_wait(barrier, len(partners))

    def quarter_of(h, c):
        return pl.ds(pl.multiple_of((h * 2 + c) * quarter, 16), quarter)

    def rows_of(cut):
        return pl.ds(cut[0], cut[1])

    def copy(src, dst, number, device, number_there=None):
        there = number if number_there is None else number_there
        return pltpu.make_async_remote_copy(
            src_ref=src, dst_ref=dst, send_sem=send.at[number], recv_sem=recv.at[there],
            device_id=device, device_id_type=MESH,
        )

    table_up = [copy(tab_hbm.at[rows_of(c)], arr.at[rows_of(c)], TABLE + i, up) for i, c in enumerate(TABLE_CUTS)]
    grad_up = [copy(dwp.at[rows_of(c)], dwr.at[rows_of(c)], GRAD + i, up) for i, c in enumerate(GRAD_CUTS)]

    def inside(cut):
        return pl.ds(cut[0] - LONG_FROM, cut[1])

    leg_1 = [copy(dwp.at[rows_of(c)], way_a.at[inside(c)], LONG + i, leg_to) for i, c in enumerate(LONG_CUTS)]
    leg_2 = [copy(way_a.at[inside(c)], way_b.at[inside(c)], LONG + 2 + i, turn_to) for i, c in enumerate(LONG_CUTS)]
    leg_3 = [copy(way_b.at[inside(c)], dwr.at[rows_of(c)], LONG + 4 + i, last_to) for i, c in enumerate(LONG_CUTS)]

    mine = quarter_of(hi, core)
    hidden_out = [copy(hid_hbm.at[mine], oth.at[mine], SIDE_HID + h, side[h], SIDE_HID + hi) for h in range(2)]
    hidden_in = [copy(oth.at[quarter_of(h, core)], oth.at[quarter_of(h, core)], SIDE_HID + h, side[h]) for h in range(2)]
    relay = [copy(oth.at[quarter_of(h, core)], oth.at[quarter_of(h, core)], SIDE_RELAY + h, sibling) for h in range(2)]
    aux_side = copy(aux_ref, aux_oth, AUX, at(row, 1 - lo, hi, core))
    aux_up = copy(aux_ref, aux_arr, AUX + 1, up)

    aux_side.start()
    for c in hidden_out:
        c.start()
    aux_up.start()
    for i in range(3):
        table_up[i].start()

    def spread(ref, slot):
        for i in range(ref.shape[1] // 128):
            block = ref[:, i * 128:(i + 1) * 128]
            square = jnp.concatenate([block] * 16, axis=0)
            rest = min(128, tokens - i * 128)
            cols[slot, i * 128:i * 128 + rest, :] = square.T[:rest]

    def slope(hid_ref, tab_ref, slot, base, out, out_t, start):
        group = pl.ds(start, GROUP)
        logits = lax.dot_general(
            hid_ref[...], tab_ref[group, :], (((1,), (1,)), ((), ())), preferred_element_type=F32
        )
        ids = (lax.broadcasted_iota(jnp.int32, (1, GROUP), 1) + (part * vocab + start)).astype(F32)
        hit = (cols[slot, :, 0:1] == base + ids).astype(F32)
        value = cols[slot, :, 2:3] * (jnp.exp(logits - cols[slot, :, 1:2]) - hit)
        out[:, group] = value.astype(BF16)
        out_t[group, :] = value.T.astype(BF16)

    def each_group(body):
        def step(i, carry):
            body(pl.multiple_of(i * GROUP, GROUP))
            return carry
        lax.fori_loop(0, vocab // GROUP, step, 0)

    def each_wide(body):
        def step(i, carry):
            body(pl.ds(pl.multiple_of(i * WIDE, WIDE), WIDE))
            return carry
        lax.fori_loop(0, width // WIDE, step, 0)

    def table_term(terms, start, out, dtype):
        group = pl.ds(start, GROUP)

        def body(wide):
            total = None
            for st, h in terms:
                term = jnp.dot(st[group, :], h[:, wide], preferred_element_type=F32)
                total = term if total is None else total + term
            out[group, wide] = total.astype(dtype)
        each_wide(body)

    def hidden_term(terms, rows, store):
        def body(wide):
            total = None
            for s, t, span in terms:
                term = jnp.dot(s[rows, span], t[span, wide], preferred_element_type=F32)
                total = term if total is None else total + term
            store(wide, total)
        each_wide(body)

    def core_copy(tok, h):
        slot = tok * 2 + h
        return copy(cc_out.at[slot], cc_in.at[slot], CORE + slot, sibling)

    def begin(tok, terms):
        for h in range(2):
            for c, place in ((1 - core, give), (core, keep)):
                def put(wide, value, place=place, slot=tok * 2 + h):
                    place[slot, :, wide] = value
                hidden_term(terms, quarter_of(h, c), put)

    def halve(tok, terms, begun):
        for h in range(2):
            def put(wide, value, slot=tok * 2 + h):
                if begun:
                    value = value + give[slot, :, wide]
                cc_out[slot, :, wide] = value.astype(BF16)
            hidden_term(terms, quarter_of(h, 1 - core), put)
            core_copy(tok, h).start()
        for h in range(2):
            def put(wide, value, slot=tok * 2 + h):
                if begun:
                    value = value + keep[slot, :, wide]
                keep[slot, :, wide] = value
            hidden_term(terms, quarter_of(h, core), put)

    def x_copy(slot, dst_slot, device):
        return copy(x_out.at[slot], x_in.at[dst_slot], ACROSS + slot, device, ACROSS + dst_slot)

    def send_other():
        for h in range(2):
            core_copy(1, h).wait_recv()
            x_out[1 + h] = (keep[2 + h] + cc_in[2 + h].astype(F32)).astype(BF16)
            x_copy(1 + h, 1 + hi, side[h]).start()

    whole, first, second = pl.ds(0, vocab), pl.ds(0, GROUP), pl.ds(GROUP, GROUP)

    spread(aux_ref, 0)
    load_hid.wait()
    load_tab.wait()
    base_own = aux_ref[3:4, 0:1]
    each_group(lambda start: slope(hid, tab, 0, base_own, s_own, t_own, start))

    table_up[0].wait_send()
    table_up[3].start()
    for h in range(2):
        hidden_in[h].wait_recv()
        relay[h].start()
    aux_side.wait_recv()
    spread(aux_oth, 1)
    for h in range(2):
        relay[h].wait_recv()
    for i in range(1, 3):
        table_up[i].wait_send()
        table_up[i + 3].start()

    @pl.when(lo == 0)
    def _():
        each_group(lambda start: slope(oth, tab, 1, base_own, s_oth, t_oth, start))
        table_term([(t_own, hid), (t_oth, oth)], GROUP, dwp, BF16)
        for c in leg_1:
            c.start()
        halve(1, [(s_oth, tab, whole)], False)
        send_other()
        table_term([(t_own, hid), (t_oth, oth)], 0, dwp, BF16)

    @pl.when(lo == 1)
    def _():
        table_term([(t_own, hid)], GROUP, dwp, BF16)
        for c in leg_1:
            c.start()
        table_term([(t_own, hid)], 0, dwp, BF16)

    for i in range(3, 5):
        table_up[i].wait_send()
        table_up[i + 3].start()

    aux_up.wait_recv()
    base_arr = aux_arr[3:4, 0:1]
    for i in range(4):
        table_up[i].wait_recv()
    slope(hid, arr, 0, base_arr, s_arr, t_arr, 0)

    @pl.when(lo == 0)
    def _():
        begin(0, [(s_own, tab, whole), (s_arr, arr, first)])
        table_term([(t_arr, hid)], 0, grad, F32)

    @pl.when(lo == 1)
    def _():
        slope(oth, arr, 1, base_arr, s_oth, t_oth, 0)
        begin(1, [(s_oth, arr, first)])
        begin(0, [(s_own, tab, whole), (s_arr, arr, first)])
        table_term([(t_arr, hid), (t_oth, oth)], 0, grad, F32)

    leg_1[0].wait_recv()
    leg_2[0].start()
    for i in range(5, 8):
        table_up[i].wait_send()
    for i in range(3):
        grad_up[i].start()

    for i in range(4, 8):
        table_up[i].wait_recv()

    @pl.when(lo == 1)
    def _():
        slope(oth, arr, 1, base_arr, s_oth, t_oth, GROUP)
        halve(1, [(s_oth, arr, second)], True)

    leg_1[1].wait_recv()
    leg_2[1].start()
    slope(hid, arr, 0, base_arr, s_arr, t_arr, GROUP)

    @pl.when(lo == 1)
    def _():
        send_other()

    halve(0, [(s_arr, arr, second)], True)
    for h in range(2):
        core_copy(0, h).wait_recv()
    x_out[0] = (keep[1 - hi] + cc_in[1 - hi].astype(F32)).astype(BF16)
    x_copy(0, 0, across).start()
    grad_up[0].wait_send()
    grad_up[3].start()

    @pl.when(lo == 0)
    def _():
        table_term([(t_arr, hid)], GROUP, grad, F32)

    @pl.when(lo == 1)
    def _():
        table_term([(t_arr, hid), (t_oth, oth)], GROUP, grad, F32)

    def finish(cut):
        grad[rows_of(cut)] = grad[rows_of(cut)] + dwr[rows_of(cut)].astype(F32)

    count = len(GRAD_CUTS)
    leg_2[0].wait_recv()
    leg_3[0].start()
    for i in range(count):
        if i + 4 < count:
            grad_up[i + 1].wait_send()
            grad_up[i + 4].start()
        if i == 2:
            leg_2[1].wait_recv()
            leg_3[1].start()
        if i < count - 1:
            grad_up[i].wait_recv()
            finish(GRAD_CUTS[i])
    for i in range(2):
        leg_3[i].wait_recv()
        finish(LONG_CUTS[i])
    for slot, device in ((0, across), (1, side[0]), (2, side[1])):
        x_copy(slot, slot, device).wait_recv()
    total = keep[hi] + cc_in[hi].astype(F32)
    for slot in range(3):
        total = total + x_in[slot].astype(F32)
    gh_out[...] = total.astype(BF16)
    grad_up[count - 1].wait_recv()
    finish(GRAD_CUTS[count - 1])

    aux_side.wait_send()
    aux_up.wait_send()
    for c in hidden_out + relay + leg_1 + leg_2 + leg_3 + grad_up[count - 3:]:
        c.wait_send()
    for tok in range(2):
        for h in range(2):
            core_copy(tok, h).wait_send()
    for slot, device in ((0, across), (1, side[0]), (2, side[1])):
        x_copy(slot, slot, device).wait_send()


def per_device(rows_of_ring, hidden, table, targets, group_start, log_norm, loss_grad):
    tokens, width = hidden.shape
    vocab = table.shape[0]
    quarter = tokens // 4
    padded = -(-tokens // 128) * 128
    dma = pltpu.SemaphoreType.DMA
    return pl.pallas_call(
        functools.partial(kernel, rows_of_ring),
        out_shape=(
            pltpu.VMEM((quarter, width), BF16),
            pltpu.VMEM((vocab, width), F32),
        ),
        in_specs=[
            pl.BlockSpec(memory_space=pltpu.VMEM),
            pl.BlockSpec(memory_space=pltpu.SMEM),
            pl.BlockSpec(memory_space=pltpu.VMEM),
            pl.BlockSpec(memory_space=pltpu.VMEM),
            pl.BlockSpec(memory_space=pl.ANY),
            pl.BlockSpec(memory_space=pl.ANY),
        ],
        out_specs=[pl.BlockSpec(memory_space=pltpu.VMEM)] * 2,
        scratch_shapes=[
            *[pltpu.VMEM((tokens, width), BF16)] * 2,
            *[pltpu.VMEM((vocab, width), BF16)] * 2,
            *[pltpu.VMEM((8, padded), F32)] * 3,
            pltpu.VMEM((2, tokens, 128), F32),
            *[pltpu.VMEM((tokens, vocab), BF16)] * 3,
            *[pltpu.VMEM((vocab, tokens), BF16)] * 3,
            *[pltpu.VMEM((vocab, width), BF16)] * 2,
            *[pltpu.VMEM((4, quarter, width), F32)] * 2,
            *[pltpu.VMEM((4, quarter, width), BF16)] * 2,
            *[pltpu.VMEM((3, quarter, width), BF16)] * 2,
            *[pltpu.VMEM((vocab - LONG_FROM, width), BF16)] * 2,
            dma((2,)), dma((COPIES,)), dma((COPIES,)),
        ],
        compiler_params=pltpu.CompilerParams(
            collective_id=1, has_side_effects=True, vmem_limit_bytes=56 * 2**20
        ),
        cost_estimate=pl.CostEstimate(
            flops=18 * tokens * vocab * width, bytes_accessed=12 * tokens * width, transcendentals=3 * tokens * vocab
        ),
    )(targets, group_start, log_norm, loss_grad, hidden, table)


def solution(mesh):
    placed = (P("blk", None), P(("blk", "vocab"), None), P("blk"), P("blk"), P("blk"), P("blk"))
    return jax.shard_map(
        functools.partial(per_device, mesh.shape["blk"] // 2),
        mesh=mesh,
        in_specs=placed,
        out_specs=(P(("blk", "vocab"), None), P(("blk", "vocab"), None)),
        check_vma=False,
    )
```

time: 127 us -> 112 us (0.88)
  Pallas kernels: 116 us -> 107 us
  local copies, waits for them, and re-layouts: 8.98 us -> 3.08 us
    pallas_call x1, Pallas kernels: 116 us -> 107 us  [per_device(): pl.pallas_call(functools.partial(kernel, rows_of_ring), out_shape=(pltpu....]
    unnamed x2, local copies, waits for them, and re-layouts: 6.91 us -> 3.08 us
    another operation x4 -> x0, local copies, waits for them, and re-layouts: 1.46 us -> none  [per_device(): jnp.stack([targets.astype(F32), log_norm, loss_grad, jnp.broadcast_to(gro...]
where the time goes in v2:
time: 112 us; the launch traced here: 111 us
  Pallas kernels  107 us (96%)
  local copies, waits for them, and re-layouts  3.08 us (3%)
  between operations  1.29 us (1%)
    pallas_call x1, Pallas kernels, per_device(): pl.pallas_call(functools.partial(kernel, rows_of_ring), out_shape=(pltpu....  107 us
    unnamed x2, local copies, waits for them, and re-layouts  3.08 us

profile of v2, /device:TPU:1, one launch (start us, length us, event | category | flops | bytes accessed | tf_op | source)
XLA Modules:
  0.0 111.4 jit_solution(6104841870963292698)
XLA Ops:
  1.3 107.1 %shard_map.77 = (bf16[176,2304]{1,0:T(8,128)(2,1)S(1)}, f32[512,2304]{1,0:T(8,128)S(1)}) custom-call(s32[704]{0:T(1024)} %tgt_ref.1, s32[1]{0:T(128)S(6)} %copy.12.first_ref, f32[704]{0:T(1024)} %norm_ref.1, f32[704]{0:T(1024)} %cot_ref.1, bf16[704,2304]{1,0:T(8,128)(2,1)} %hid_hbm.1, bf16[512,2304]{1,0:T(8,128)(2,1)} %tab_hbm.1), custom_call_target="tpu_custom_call" | custom-call | flops 14948499456 | bytes 19464192 | tf_op jit(solution)/shard_map/pallas_call | solution.py:343
  108.3 0.9 copy.10
  109.2 2.2 %copy.11 = f32[512,2304]{1,0:T(8,128)} copy(f32[512,2304]{1,0:T(8,128)S(1)} %get-tuple-element.3) | data formatting | bytes 9437184

commit v3 on v2

--- a/solution.py
+++ b/solution.py
@@ -12,23 +12,33 @@
 WIDE = 768
 RING, LEG = 8, 3
 TABLE_CUTS = tuple((64 * i, 64) for i in range(8))
-GRAD_CUTS = tuple((64 * i, 64) for i in range(6)) + ((384, 48),)
-LONG_FROM = 432
+GRAD_CUTS = tuple((64 * i, 64) for i in range(5)) + ((320, 16),)
+SIDE_CUTS = ((336, 48), (384, 48))
 LONG_CUTS = ((432, 48), (480, 32))
+SIDE_PARTS = ((0, 0, 32), (1, 0, 32), (0, 32, 16), (1, 32, 16))
+LONG_ROWS = 112
+HID_CUTS = ((0, 0, 64), (0, 64, 64), (0, 128, 48), (1, 0, 64))
+HID_LONG = ((1, 64, 64), (1, 128, 48))
+HID_SHARE = ((0, 0, 176), (1, 0, 64)) + HID_LONG
 F32, BF16 = jnp.float32, jnp.bfloat16
 
-AUX, SIDE_HID, SIDE_RELAY, CORE, ACROSS = 0, 2, 4, 6, 10
-TABLE = 13
+AUX, SIDE_HID, SIDE_RELAY, CORE, CROSS, SIDE = 0, 2, 4, 6, 10, 12
+TABLE = 16
 GRAD = TABLE + len(TABLE_CUTS)
 LONG = GRAD + len(GRAD_CUTS)
-COPIES = LONG + 6
+HID_UP = LONG + 6
+HID_RELAY = HID_UP + len(HID_CUTS)
+BY_SIDE = HID_RELAY + len(HID_SHARE)
+BY_UP = BY_SIDE + 2
+BY_BACK = BY_UP + 4
+COPIES = BY_BACK + 4
 
 
 def kernel(
     rows_of_ring, tgt_ref, first_ref, norm_ref, cot_ref, hid_hbm, tab_hbm, gh_out, grad,
-    hid, oth, tab, arr, aux_ref, aux_oth, aux_arr, cols,
-    s_own, s_oth, s_arr, t_own, t_oth, t_arr,
-    dwp, dwr, keep, give, cc_out, cc_in, x_out, x_in, way_a, way_b, lsem, send, recv,
+    hid, oth, thr, tab, arr, aux_ref, aux_oth, aux_arr, cols,
+    s_own, s_oth, s_arr, t_own, t_oth, t_arr, t_thr,
+    dwp, dwr, keep, give, cc_out, cc_in, x_out, x_in, m_in, way_a, way_b, by_in, by_up, lsem, send, recv,
 ):
     tokens, width = hid.shape
     vocab = tab.shape[0]
@@ -45,7 +55,6 @@
         return y * RING + (z + RING) % RING
 
     up, down = at(row + 1, lo, hi, core), at(row - 1, lo, hi, core)
-    across = at(row, lo, 1 - hi, core)
     side = [at(row, 1 - lo, h, core) for h in range(2)]
     sibling = at(row, lo, hi, 1 - core)
     turn_to = lax.rem(height + RING + LEG, RING) == RING - 1
@@ -57,6 +66,11 @@
     last_to = at(along(plane, height - 1), lo, hi, core)
     last_from = at(along(plane, height + 1), lo, hi, core)
 
+    barrier = pltpu.get_barrier_semaphore()
+    partners = (up, down, side[0], side[1], sibling, leg_to, leg_from, turn_to, turn_from, last_to, last_from)
+    for device in partners:
+        pl.semaphore_signal(barrier, inc=1, device_id=device, device_id_type=MESH)
+
     load_hid = pltpu.make_async_copy(hid_hbm, hid, lsem.at[0])
     load_tab = pltpu.make_async_copy(tab_hbm, tab, lsem.at[1])
     load_hid.start()
@@ -68,10 +82,6 @@
     aux_ref[2:3, :tokens] = cot_ref[...].reshape(1, tokens)
     aux_ref[3:4, :] = jnp.full((1, aux_ref.shape[1]), first_ref[0].astype(F32), F32)
 
-    barrier = pltpu.get_barrier_semaphore()
-    partners = (up, down, across, side[0], side[1], sibling, leg_to, leg_from, turn_to, turn_from, last_to, last_from)
-    for device in partners:
-        pl.semaphore_signal(barrier, inc=1, device_id=device, device_id_type=MESH)
     pl.semaphore_wait(barrier, len(partners))
 
     def quarter_of(h, c):
@@ -90,12 +100,40 @@
     table_up = [copy(tab_hbm.at[rows_of(c)], arr.at[rows_of(c)], TABLE + i, up) for i, c in enumerate(TABLE_CUTS)]
     grad_up = [copy(dwp.at[rows_of(c)], dwr.at[rows_of(c)], GRAD + i, up) for i, c in enumerate(GRAD_CUTS)]
 
-    def inside(cut):
-        return pl.ds(cut[0] - LONG_FROM, cut[1])
-
-    leg_1 = [copy(dwp.at[rows_of(c)], way_a.at[inside(c)], LONG + i, leg_to) for i, c in enumerate(LONG_CUTS)]
-    leg_2 = [copy(way_a.at[inside(c)], way_b.at[inside(c)], LONG + 2 + i, turn_to) for i, c in enumerate(LONG_CUTS)]
-    leg_3 = [copy(way_b.at[inside(c)], dwr.at[rows_of(c)], LONG + 4 + i, last_to) for i, c in enumerate(LONG_CUTS)]
+    def piece_of(cut):
+        return pl.ds(pl.multiple_of((cut[0] * 2 + core) * quarter + cut[1], 16), cut[2])
+
+    def legs(sources, targets, sizes):
+        first, second, third, place = [], [], [], 0
+        for i, (source, target, size) in enumerate(zip(sources, targets, sizes)):
+            stop = pl.ds(place, size)
+            first.append(copy(source, way_a.at[stop], LONG + i, leg_to))
+            second.append(copy(way_a.at[stop], way_b.at[stop], LONG + 2 + i, turn_to))
+            third.append(copy(way_b.at[stop], target, LONG + 4 + i, last_to))
+            place += size
+        return first, second, third
+
+    leg_1, leg_2, leg_3 = legs(
+        [dwp.at[rows_of(c)] for c in LONG_CUTS], [dwr.at[rows_of(c)] for c in LONG_CUTS], [c[1] for c in LONG_CUTS]
+    )
+    leg_1_odd, leg_2_odd, leg_3_odd = legs(
+        [hid_hbm.at[piece_of(h)] for h in HID_LONG], [thr.at[piece_of(h)] for h in HID_LONG], [h[2] for h in HID_LONG]
+    )
+
+    hid_up = [copy(hid_hbm.at[piece_of(h)], thr.at[piece_of(h)], HID_UP + i, up) for i, h in enumerate(HID_CUTS)]
+    hid_relay = [copy(thr.at[piece_of(h)], thr.at[piece_of(h)], HID_RELAY + i, sibling) for i, h in enumerate(HID_SHARE)]
+
+    by_side = [copy(dwp.at[rows_of(c)], by_in.at[hi], BY_SIDE + g, side[g], BY_SIDE + hi) for g, c in enumerate(SIDE_CUTS)]
+    by_side_in = [copy(by_in.at[h], by_in.at[h], BY_SIDE + h, side[h]) for h in range(2)]
+    by_above, by_back, by_back_in = [], [], []
+    for j, (h, low, size) in enumerate(SIDE_PARTS):
+        there = SIDE_CUTS[0][0] + low
+        rows = pl.ds(low, size)
+        back = pl.ds(pl.multiple_of(there + hi * SIDE_CUTS[0][1], 16), size)
+        by_above.append(copy(by_in.at[h, rows], by_up.at[h, rows], BY_UP + j, up))
+        by_back.append(copy(by_up.at[h, rows], dwr.at[back], BY_BACK + j, side[h], BY_BACK + 2 * (j // 2) + hi))
+        landed = pl.ds(there + h * SIDE_CUTS[0][1], size)
+        by_back_in.append(copy(by_up.at[h, rows], dwr.at[landed], BY_BACK + j, side[h]))
 
     mine = quarter_of(hi, core)
     hidden_out = [copy(hid_hbm.at[mine], oth.at[mine], SIDE_HID + h, side[h], SIDE_HID + hi) for h in range(2)]
@@ -110,6 +148,11 @@
     aux_up.start()
     for i in range(3):
         table_up[i].start()
+
+    @pl.when(lo == 1)
+    def _():
+        for c in leg_1_odd:
+            c.start()
 
     def spread(ref, slot):
         for i in range(ref.shape[1] // 128):
@@ -126,7 +169,8 @@
         ids = (lax.broadcasted_iota(jnp.int32, (1, GROUP), 1) + (part * vocab + start)).astype(F32)
         hit = (cols[slot, :, 0:1] == base + ids).astype(F32)
         value = cols[slot, :, 2:3] * (jnp.exp(logits - cols[slot, :, 1:2]) - hit)
-        out[:, group] = value.astype(BF16)
+        if out is not None:
+            out[:, group] = value.astype(BF16)
         out_t[group, :] = value.T.astype(BF16)
 
     def each_group(body):
@@ -141,11 +185,11 @@
             return carry
         lax.fori_loop(0, width // WIDE, step, 0)
 
-    def table_term(terms, start, out, dtype):
+    def table_term(terms, start, out, dtype, more=False):
         group = pl.ds(start, GROUP)
 
         def body(wide):
-            total = None
+            total = out[group, wide] if more else None
             for st, h in terms:
                 term = jnp.dot(st[group, :], h[:, wide], preferred_element_type=F32)
                 total = term if total is None else total + term
@@ -187,14 +231,48 @@
                 keep[slot, :, wide] = value
             hidden_term(terms, quarter_of(h, core), put)
 
-    def x_copy(slot, dst_slot, device):
-        return copy(x_out.at[slot], x_in.at[dst_slot], ACROSS + slot, device, ACROSS + dst_slot)
+    half = width // 2
+
+    def columns(g):
+        return pl.ds(pl.multiple_of(g * half, 128), half)
+
+    def cross_copy(g):
+        return copy(x_out.at[0, :, columns(g)], m_in.at[hi], CROSS + g, side[g], CROSS + hi)
+
+    def cross_arrival(g):
+        return copy(x_out.at[0, :, columns(g)], m_in.at[g], CROSS + g, side[g])
+
+    def side_copy(h, late):
+        span = columns(hi if late else 1 - hi)
+        return copy(
+            x_out.at[1 + h, :, span], x_in.at[hi, :, span], SIDE + 2 * h + late, side[h], SIDE + 2 * hi + late
+        )
+
+    def side_arrival(h, late):
+        span = columns(h if late else 1 - h)
+        return copy(x_out.at[1 + h, :, span], x_in.at[h, :, span], SIDE + 2 * h + late, side[h])
+
+    def send_own():
+        for h in range(2):
+            core_copy(0, h).wait_recv()
+        x_out[0] = (keep[1 - hi] + cc_in[1 - hi].astype(F32)).astype(BF16)
+        for g in range(2):
+            cross_copy(g).start()
 
     def send_other():
         for h in range(2):
             core_copy(1, h).wait_recv()
-            x_out[1 + h] = (keep[2 + h] + cc_in[2 + h].astype(F32)).astype(BF16)
-            x_copy(1 + h, 1 + hi, side[h]).start()
+            span = columns(1 - hi)
+            x_out[1 + h, :, span] = (keep[2 + h, :, span] + cc_in[2 + h, :, span].astype(F32)).astype(BF16)
+            side_copy(h, 0).start()
+
+    def send_rest():
+        for h in range(2):
+            cross_arrival(1 - h).wait_recv()
+            span = columns(hi)
+            value = keep[2 + h, :, span] + cc_in[2 + h, :, span].astype(F32) + m_in[1 - h].astype(F32)
+            x_out[1 + h, :, span] = value.astype(BF16)
+            side_copy(h, 1).start()
 
     whole, first, second = pl.ds(0, vocab), pl.ds(0, GROUP), pl.ds(GROUP, GROUP)
 
@@ -221,7 +299,7 @@
     def _():
         each_group(lambda start: slope(oth, tab, 1, base_own, s_oth, t_oth, start))
         table_term([(t_own, hid), (t_oth, oth)], GROUP, dwp, BF16)
-        for c in leg_1:
+        for c in by_side + leg_1:
             c.start()
         halve(1, [(s_oth, tab, whole)], False)
         send_other()
@@ -229,14 +307,17 @@
 
     @pl.when(lo == 1)
     def _():
-        table_term([(t_own, hid)], GROUP, dwp, BF16)
-        for c in leg_1:
-            c.start()
-        table_term([(t_own, hid)], 0, dwp, BF16)
+        leg_1_odd[0].wait_recv()
+        leg_2_odd[0].start()
 
     for i in range(3, 5):
         table_up[i].wait_send()
         table_up[i + 3].start()
+
+    @pl.when(lo == 1)
+    def _():
+        leg_1_odd[1].wait_recv()
+        leg_2_odd[1].start()
 
     aux_up.wait_recv()
     base_arr = aux_arr[3:4, 0:1]
@@ -256,82 +337,132 @@
         begin(0, [(s_own, tab, whole), (s_arr, arr, first)])
         table_term([(t_arr, hid), (t_oth, oth)], 0, grad, F32)
 
-    leg_1[0].wait_recv()
-    leg_2[0].start()
-    for i in range(5, 8):
-        table_up[i].wait_send()
-    for i in range(3):
-        grad_up[i].start()
+    @pl.when(lo == 0)
+    def _():
+        leg_1[0].wait_recv()
+        leg_2[0].start()
+        for i in range(5, 8):
+            table_up[i].wait_send()
+        for i in range(3):
+            grad_up[i].start()
+        leg_1[1].wait_recv()
+        leg_2[1].start()
+
+    @pl.when(lo == 1)
+    def _():
+        spread(aux_arr, 2)
+        for i in range(5, 8):
+            table_up[i].wait_send()
+        for c in hid_up:
+            c.start()
 
     for i in range(4, 8):
         table_up[i].wait_recv()
+    slope(hid, arr, 0, base_arr, s_arr, t_arr, GROUP)
+    halve(0, [(s_arr, arr, second)], True)
+    send_own()
 
     @pl.when(lo == 1)
     def _():
         slope(oth, arr, 1, base_arr, s_oth, t_oth, GROUP)
         halve(1, [(s_oth, arr, second)], True)
-
-    leg_1[1].wait_recv()
-    leg_2[1].start()
-    slope(hid, arr, 0, base_arr, s_arr, t_arr, GROUP)
-
-    @pl.when(lo == 1)
-    def _():
         send_other()
-
-    halve(0, [(s_arr, arr, second)], True)
-    for h in range(2):
-        core_copy(0, h).wait_recv()
-    x_out[0] = (keep[1 - hi] + cc_in[1 - hi].astype(F32)).astype(BF16)
-    x_copy(0, 0, across).start()
-    grad_up[0].wait_send()
-    grad_up[3].start()
+        leg_2_odd[0].wait_recv()
+        leg_3_odd[0].start()
 
     @pl.when(lo == 0)
     def _():
+        grad_up[0].wait_send()
+        grad_up[3].start()
         table_term([(t_arr, hid)], GROUP, grad, F32)
 
     @pl.when(lo == 1)
     def _():
         table_term([(t_arr, hid), (t_oth, oth)], GROUP, grad, F32)
+
+    send_rest()
 
     def finish(cut):
         grad[rows_of(cut)] = grad[rows_of(cut)] + dwr[rows_of(cut)].astype(F32)
 
-    count = len(GRAD_CUTS)
-    leg_2[0].wait_recv()
-    leg_3[0].start()
-    for i in range(count):
-        if i + 4 < count:
-            grad_up[i + 1].wait_send()
-            grad_up[i + 4].start()
-        if i == 2:
-            leg_2[1].wait_recv()
-            leg_3[1].start()
-        if i < count - 1:
+    def finish_hidden():
+        for h in range(2):
+            for late in range(2):
+                side_arrival(h, late).wait_recv()
+        total = keep[hi] + cc_in[hi].astype(F32) + x_in[0].astype(F32) + x_in[1].astype(F32)
+        gh_out[...] = total.astype(BF16)
+
+    @pl.when(lo == 0)
+    def _():
+        count = len(GRAD_CUTS)
+        leg_2[0].wait_recv()
+        leg_3[0].start()
+        for i in range(count):
+            if i + 4 < count:
+                grad_up[i + 1].wait_send()
+                grad_up[i + 4].start()
+            if i == 2:
+                leg_2[1].wait_recv()
+                leg_3[1].start()
             grad_up[i].wait_recv()
             finish(GRAD_CUTS[i])
-    for i in range(2):
-        leg_3[i].wait_recv()
-        finish(LONG_CUTS[i])
-    for slot, device in ((0, across), (1, side[0]), (2, side[1])):
-        x_copy(slot, slot, device).wait_recv()
-    total = keep[hi] + cc_in[hi].astype(F32)
-    for slot in range(3):
-        total = total + x_in[slot].astype(F32)
-    gh_out[...] = total.astype(BF16)
-    grad_up[count - 1].wait_recv()
-    finish(GRAD_CUTS[count - 1])
+        for i in range(2):
+            leg_3[i].wait_recv()
+            finish(LONG_CUTS[i])
+        finish_hidden()
+        for j, (h, low, size) in enumerate(SIDE_PARTS):
+            by_back_in[j].wait_recv()
+            finish((SIDE_CUTS[h][0] + low, size))
+        for c in by_side + leg_1 + leg_2 + leg_3 + grad_up[count - 3:]:
+            c.wait_send()
+
+    @pl.when(lo == 1)
+    def _():
+        for c in by_side_in:
+            c.wait_recv()
+        hid_up[0].wait_send()
+        hid_up[1].wait_send()
+        by_above[0].start()
+        leg_2_odd[1].wait_recv()
+        leg_3_odd[1].start()
+        hid_up[2].wait_send()
+        by_above[1].start()
+        for c in hid_up[:3]:
+            c.wait_recv()
+        hid_relay[0].start()
+        for i in range(2):
+            leg_3_odd[i].wait_recv()
+            hid_relay[2 + i].start()
+        hid_up[3].wait_send()
+        by_above[2].start()
+        by_above[3].start()
+        hid_up[3].wait_recv()
+        hid_relay[1].start()
+        for j in range(2):
+            by_above[j].wait_recv()
+            by_back[j].start()
+        for c in hid_relay:
+            c.wait_recv()
+        each_group(lambda start: slope(thr, arr, 2, base_arr, None, t_thr, start))
+        for j in range(2, 4):
+            by_above[j].wait_recv()
+            by_back[j].start()
+        each_group(lambda start: table_term([(t_thr, thr)], start, grad, F32, more=True))
+        finish_hidden()
+        for c in leg_1_odd + leg_2_odd + leg_3_odd + hid_relay + by_back + by_above:
+            c.wait_send()
 
     aux_side.wait_send()
     aux_up.wait_send()
-    for c in hidden_out + relay + leg_1 + leg_2 + leg_3 + grad_up[count - 3:]:
+    for c in hidden_out + relay:
         c.wait_send()
     for tok in range(2):
         for h in range(2):
             core_copy(tok, h).wait_send()
-    for slot, device in ((0, across), (1, side[0]), (2, side[1])):
-        x_copy(slot, slot, device).wait_send()
+    for h in range(2):
+        cross_arrival(h).wait_send()
+        for late in range(2):
+            side_arrival(h, late).wait_send()
 
 
 def per_device(rows_of_ring, hidden, table, targets, group_start, log_norm, loss_grad):
@@ -356,17 +487,20 @@
         ],
         out_specs=[pl.BlockSpec(memory_space=pltpu.VMEM)] * 2,
         scratch_shapes=[
-            *[pltpu.VMEM((tokens, width), BF16)] * 2,
+            *[pltpu.VMEM((tokens, width), BF16)] * 3,
             *[pltpu.VMEM((vocab, width), BF16)] * 2,
             *[pltpu.VMEM((8, padded), F32)] * 3,
-            pltpu.VMEM((2, tokens, 128), F32),
+            pltpu.VMEM((3, tokens, 128), F32),
             *[pltpu.VMEM((tokens, vocab), BF16)] * 3,
-            *[pltpu.VMEM((vocab, tokens), BF16)] * 3,
+            *[pltpu.VMEM((vocab, tokens), BF16)] * 4,
             *[pltpu.VMEM((vocab, width), BF16)] * 2,
             *[pltpu.VMEM((4, quarter, width), F32)] * 2,
             *[pltpu.VMEM((4, quarter, width), BF16)] * 2,
-            *[pltpu.VMEM((3, quarter, width), BF16)] * 2,
-            *[pltpu.VMEM((vocab - LONG_FROM, width), BF16)] * 2,
+            pltpu.VMEM((3, quarter, width), BF16),
+            pltpu.VMEM((2, quarter, width), BF16),
+            pltpu.VMEM((2, quarter, width // 2), BF16),
+            *[pltpu.VMEM((LONG_ROWS, width), BF16)] * 2,
+            *[pltpu.VMEM((2, SIDE_CUTS[0][1], width), BF16)] * 2,
             dma((2,)), dma((COPIES,)), dma((COPIES,)),
         ],
         compiler_params=pltpu.CompilerParams(

time: 112 us -> 108 us (0.964)
  Pallas kernels: 107 us -> 104 us
    pallas_call x1, Pallas kernels: 107 us -> 104 us  [per_device(): pl.pallas_call(functools.partial(kernel, rows_of_ring), out_shape=(pltpu....]
where the time goes in v3:
time: 108 us
  Pallas kernels  104 us (96%)
  local copies, waits for them, and re-layouts  3.08 us (3%)
  between operations  1.29 us (1%)
    pallas_call x1, Pallas kernels, per_device(): pl.pallas_call(functools.partial(kernel, rows_of_ring), out_shape=(pltpu....  104 us
    unnamed x2, local copies, waits for them, and re-layouts  3.08 us

profile of v3, /device:TPU:1, one launch (start us, length us, event | category | flops | bytes accessed | tf_op | source)
XLA Modules:
  0.0 108.4 jit_solution(13673352016106161306)
XLA Ops:
  1.3 104.0 %shard_map.77 = (bf16[176,2304]{1,0:T(8,128)(2,1)S(1)}, f32[512,2304]{1,0:T(8,128)S(1)}) custom-call(s32[704]{0:T(1024)} %tgt_ref.1, s32[1]{0:T(128)S(6)} %copy.12.first_ref, f32[704]{0:T(1024)} %norm_ref.1, f32[704]{0:T(1024)} %cot_ref.1, bf16[704,2304]{1,0:T(8,128)(2,1)} %hid_hbm.1, bf16[512,2304]{1,0:T(8,128)(2,1)} %tab_hbm.1), custom_call_target="tpu_custom_call" | custom-call | flops 14948499456 | bytes 19464192 | tf_op jit(solution)/shard_map/pallas_call | solution.py:474
  105.3 0.9 copy.10
  106.2 2.2 %copy.11 = f32[512,2304]{1,0:T(8,128)} copy(f32[512,2304]{1,0:T(8,128)S(1)} %get-tuple-element.3) | data formatting | bytes 9437184

commit v4 on v3

--- a/solution.py
+++ b/solution.py
@@ -12,10 +12,11 @@
 WIDE = 768
 RING, LEG = 8, 3
 TABLE_CUTS = tuple((64 * i, 64) for i in range(8))
-GRAD_CUTS = tuple((64 * i, 64) for i in range(5)) + ((320, 16),)
-SIDE_CUTS = ((336, 48), (384, 48))
+GRAD_CUTS = tuple((64 * i, 64) for i in range(5)) + ((320, 48),)
+SIDE_CUTS = ((368, 32), (400, 32))
 LONG_CUTS = ((432, 48), (480, 32))
-SIDE_PARTS = ((0, 0, 32), (1, 0, 32), (0, 32, 16), (1, 32, 16))
+SIDE_PARTS = ((0, 0, 32), (1, 0, 32))
+LONG_TABLE = (496, 16)
 LONG_ROWS = 112
 HID_CUTS = ((0, 0, 64), (0, 64, 64), (0, 128, 48), (1, 0, 64))
 HID_LONG = ((1, 64, 64), (1, 128, 48))
@@ -30,8 +31,9 @@
 HID_RELAY = HID_UP + len(HID_CUTS)
 BY_SIDE = HID_RELAY + len(HID_SHARE)
 BY_UP = BY_SIDE + 2
-BY_BACK = BY_UP + 4
-COPIES = BY_BACK + 4
+BY_BACK = BY_UP + 2
+LONG_TAB = BY_BACK + 2
+COPIES = LONG_TAB + 3
 
 
 def kernel(
@@ -120,6 +122,14 @@
         [hid_hbm.at[piece_of(h)] for h in HID_LONG], [thr.at[piece_of(h)] for h in HID_LONG], [h[2] for h in HID_LONG]
     )
 
+    last = TABLE_CUTS[-1][0]
+    rest = pl.ds(last, LONG_TABLE[0] - last)
+    table_last = copy(tab_hbm.at[rest], arr.at[rest], TABLE + len(TABLE_CUTS) - 1, up)
+    spare = pl.ds(LONG_ROWS - LONG_TABLE[1], LONG_TABLE[1])
+    table_1 = copy(tab_hbm.at[rows_of(LONG_TABLE)], way_a.at[spare], LONG_TAB, leg_to)
+    table_2 = copy(way_a.at[spare], way_b.at[spare], LONG_TAB + 1, turn_to)
+    table_3 = copy(way_b.at[spare], arr.at[rows_of(LONG_TABLE)], LONG_TAB + 2, last_to)
+
     hid_up = [copy(hid_hbm.at[piece_of(h)], thr.at[piece_of(h)], HID_UP + i, up) for i, h in enumerate(HID_CUTS)]
     hid_relay = [copy(thr.at[piece_of(h)], thr.at[piece_of(h)], HID_RELAY + i, sibling) for i, h in enumerate(HID_SHARE)]
 
@@ -149,6 +159,10 @@
     for i in range(3):
         table_up[i].start()
 
+    @pl.when(lo == 0)
+    def _():
+        table_1.start()
+
     @pl.when(lo == 1)
     def _():
         for c in leg_1_odd:
@@ -161,16 +175,18 @@
             rest = min(128, tokens - i * 128)
             cols[slot, i * 128:i * 128 + rest, :] = square.T[:rest]
 
+    def slope_of(hid_rows, tab_rows, slot, rows, base, start):
+        logits = lax.dot_general(
+            hid_rows, tab_rows, (((1,), (1,)), ((), ())), preferred_element_type=F32
+        )
+        ids = (lax.broadcasted_iota(jnp.int32, (1, GROUP), 1) + (part * vocab + start)).astype(F32)
+        hit = (cols[slot, rows, 0:1] == base + ids).astype(F32)
+        return cols[slot, rows, 2:3] * (jnp.exp(logits - cols[slot, rows, 1:2]) - hit)
+
     def slope(hid_ref, tab_ref, slot, base, out, out_t, start):
         group = pl.ds(start, GROUP)
-        logits = lax.dot_general(
-            hid_ref[...], tab_ref[group, :], (((1,), (1,)), ((), ())), preferred_element_type=F32
-        )
-        ids = (lax.broadcasted_iota(jnp.int32, (1, GROUP), 1) + (part * vocab + start)).astype(F32)
-        hit = (cols[slot, :, 0:1] == base + ids).astype(F32)
-        value = cols[slot, :, 2:3] * (jnp.exp(logits - cols[slot, :, 1:2]) - hit)
-        if out is not None:
-            out[:, group] = value.astype(BF16)
+        value = slope_of(hid_ref[...], tab_ref[group, :], slot, pl.ds(0, tokens), base, start)
+        out[:, group] = value.astype(BF16)
         out_t[group, :] = value.T.astype(BF16)
 
     def each_group(body):
@@ -185,11 +201,11 @@
             return carry
         lax.fori_loop(0, width // WIDE, step, 0)
 
-    def table_term(terms, start, out, dtype, more=False):
+    def table_term(terms, start, out, dtype):
         group = pl.ds(start, GROUP)
 
         def body(wide):
-            total = out[group, wide] if more else None
+            total = None
             for st, h in terms:
                 term = jnp.dot(st[group, :], h[:, wide], preferred_element_type=F32)
                 total = term if total is None else total + term
@@ -297,6 +313,8 @@
 
     @pl.when(lo == 0)
     def _():
+        table_1.wait_recv()
+        table_2.start()
         each_group(lambda start: slope(oth, tab, 1, base_own, s_oth, t_oth, start))
         table_term([(t_own, hid), (t_oth, oth)], GROUP, dwp, BF16)
         for c in by_side + leg_1:
@@ -304,15 +322,26 @@
         halve(1, [(s_oth, tab, whole)], False)
         send_other()
         table_term([(t_own, hid), (t_oth, oth)], 0, dwp, BF16)
+        table_2.wait_recv()
+        table_3.start()
 
     @pl.when(lo == 1)
     def _():
         leg_1_odd[0].wait_recv()
         leg_2_odd[0].start()
 
-    for i in range(3, 5):
-        table_up[i].wait_send()
-        table_up[i + 3].start()
+    table_up[3].wait_send()
+    table_up[6].start()
+    table_up[4].wait_send()
+
+    @pl.when(lo == 0)
+    def _():
+        table_last.start()
+
+    @pl.when(lo == 1)
+    def _():
+        table_up[7].start()
+
 
     @pl.when(lo == 1)
     def _():
@@ -341,8 +370,9 @@
     def _():
         leg_1[0].wait_recv()
         leg_2[0].start()
-        for i in range(5, 8):
+        for i in range(5, 7):
             table_up[i].wait_send()
+        table_last.wait_send()
         for i in range(3):
             grad_up[i].start()
         leg_1[1].wait_recv()
@@ -353,11 +383,23 @@
         spread(aux_arr, 2)
         for i in range(5, 8):
             table_up[i].wait_send()
-        for c in hid_up:
+        for c in by_side_in:
+            c.wait_recv()
+        for c in (hid_up[0], hid_up[1], by_above[0], by_above[1]):
             c.start()
 
-    for i in range(4, 8):
+    for i in range(4, 7):
         table_up[i].wait_recv()
+
+    @pl.when(lo == 0)
+    def _():
+        table_last.wait_recv()
+        table_3.wait_recv()
+
+    @pl.when(lo == 1)
+    def _():
+        table_up[7].wait_recv()
+
     slope(hid, arr, 0, base_arr, s_arr, t_arr, GROUP)
     halve(0, [(s_arr, arr, second)], True)
     send_own()
@@ -367,6 +409,7 @@
         slope(oth, arr, 1, base_arr, s_oth, t_oth, GROUP)
         halve(1, [(s_oth, arr, second)], True)
         send_other()
+        hid_up[2].start()
         leg_2_odd[0].wait_recv()
         leg_3_odd[0].start()
 
@@ -413,42 +456,46 @@
         for j, (h, low, size) in enumerate(SIDE_PARTS):
             by_back_in[j].wait_recv()
             finish((SIDE_CUTS[h][0] + low, size))
-        for c in by_side + leg_1 + leg_2 + leg_3 + grad_up[count - 3:]:
+        for c in [table_1, table_2, table_3] + by_side + leg_1 + leg_2 + leg_3 + grad_up[count - 3:]:
             c.wait_send()
 
-    @pl.when(lo == 1)
-    def _():
-        for c in by_side_in:
-            c.wait_recv()
-        hid_up[0].wait_send()
-        hid_up[1].wait_send()
-        by_above[0].start()
+    def half_term(n):
+        rows = pl.ds(n * 2 * quarter, 2 * quarter)
+
+        def step(start):
+            group = pl.ds(start, GROUP)
+            value = slope_of(thr[rows, :], arr[group, :], 2, rows, base_arr, start)
+            t_thr[n, group, :] = value.T.astype(BF16)
+
+            def body(wide):
+                grad[group, wide] += jnp.dot(t_thr[n, group, :], thr[rows, wide], preferred_element_type=F32)
+            each_wide(body)
+        each_group(step)
+
+    @pl.when(lo == 1)
+    def _():
+        hid_up[3].start()
         leg_2_odd[1].wait_recv()
         leg_3_odd[1].start()
-        hid_up[2].wait_send()
-        by_above[1].start()
+        for j in range(2):
+            by_above[j].wait_recv()
+            by_back[j].start()
         for c in hid_up[:3]:
             c.wait_recv()
         hid_relay[0].start()
+        hid_relay[0].wait_recv()
+        half_term(0)
         for i in range(2):
             leg_3_odd[i].wait_recv()
             hid_relay[2 + i].start()
-        hid_up[3].wait_send()
-        by_above[2].start()
-        by_above[3].start()
+        finish_hidden()
         hid_up[3].wait_recv()
         hid_relay[1].start()
-        for j in range(2):
-            by_above[j].wait_recv()
-            by_back[j].start()
-        for c in hid_relay:
+        for c in hid_relay[1:]:
             c.wait_recv()
-        each_group(lambda start: slope(thr, arr, 2, base_arr, None, t_thr, start))
-        for j in range(2, 4):
-            by_above[j].wait_recv()
-            by_back[j].start()
-        each_group(lambda start: table_term([(t_thr, thr)], start, grad, F32, more=True))
-        finish_hidden()
+        half_term(1)
+        for c in hid_up:
+            c.wait_send()
         for c in leg_1_odd + leg_2_odd + leg_3_odd + hid_relay + by_back + by_above:
             c.wait_send()
 
@@ -492,7 +539,8 @@
             *[pltpu.VMEM((8, padded), F32)] * 3,
             pltpu.VMEM((3, tokens, 128), F32),
             *[pltpu.VMEM((tokens, vocab), BF16)] * 3,
-            *[pltpu.VMEM((vocab, tokens), BF16)] * 4,
+            *[pltpu.VMEM((vocab, tokens), BF16)] * 3,
+            pltpu.VMEM((2, vocab, tokens // 2), BF16),
             *[pltpu.VMEM((vocab, width), BF16)] * 2,
             *[pltpu.VMEM((4, quarter, width), F32)] * 2,
             *[pltpu.VMEM((4, quarter, width), BF16)] * 2,

time: 108 us -> 107 us (level)
  Pallas kernels: 104 us -> 102 us
    pallas_call x1, Pallas kernels: 104 us -> 102 us  [per_device(): pl.pallas_call(functools.partial(kernel, rows_of_ring), out_shape=(pltpu....]
where the time goes in v4:
time: 107 us
  Pallas kernels  102 us (95%)
  local copies, waits for them, and re-layouts  3.08 us (3%)
  between operations  1.29 us (1%)
    pallas_call x1, Pallas kernels, per_device(): pl.pallas_call(functools.partial(kernel, rows_of_ring), out_shape=(pltpu....  102 us
    unnamed x2, local copies, waits for them, and re-layouts  3.08 us

profile of v4, /device:TPU:1, one launch (start us, length us, event | category | flops | bytes accessed | tf_op | source)
XLA Modules:
  0.0 106.8 jit_solution(13403086620904020238)
XLA Ops:
  1.3 102.4 %shard_map.77 = (bf16[176,2304]{1,0:T(8,128)(2,1)S(1)}, f32[512,2304]{1,0:T(8,128)S(1)}) custom-call(s32[704]{0:T(1024)} %tgt_ref.1, s32[1]{0:T(128)S(6)} %copy.12.first_ref, f32[704]{0:T(1024)} %norm_ref.1, f32[704]{0:T(1024)} %cot_ref.1, bf16[704,2304]{1,0:T(8,128)(2,1)} %hid_hbm.1, bf16[512,2304]{1,0:T(8,128)(2,1)} %tab_hbm.1), custom_call_target="tpu_custom_call" | custom-call | flops 14948499456 | bytes 19464192 | tf_op jit(solution)/shard_map/pallas_call | solution.py:521
  103.7 0.9 copy.10
  104.6 2.2 %copy.11 = f32[512,2304]{1,0:T(8,128)} copy(f32[512,2304]{1,0:T(8,128)S(1)} %get-tuple-element.3) | data formatting | bytes 9437184

commit v5 on v4

--- a/solution.py
+++ b/solution.py
@@ -268,12 +268,26 @@
         span = columns(h if late else 1 - h)
         return copy(x_out.at[1 + h, :, span], x_in.at[h, :, span], SIDE + 2 * h + late, side[h])
 
-    def send_own():
-        for h in range(2):
-            core_copy(0, h).wait_recv()
+    def halve_own(terms):
+        def share(h):
+            def put(wide, value):
+                cc_out[h, :, wide] = (value + give[h, :, wide]).astype(BF16)
+            hidden_term(terms, quarter_of(h, 1 - core), put)
+            core_copy(0, h).start()
+
+        def hold(h):
+            def put(wide, value):
+                keep[h, :, wide] = value + keep[h, :, wide]
+            hidden_term(terms, quarter_of(h, core), put)
+
+        share(1 - hi)
+        hold(1 - hi)
+        share(hi)
+        core_copy(0, 1 - hi).wait_recv()
         x_out[0] = (keep[1 - hi] + cc_in[1 - hi].astype(F32)).astype(BF16)
         for g in range(2):
             cross_copy(g).start()
+        hold(hi)
 
     def send_other():
         for h in range(2):
@@ -317,13 +331,13 @@
         table_2.start()
         each_group(lambda start: slope(oth, tab, 1, base_own, s_oth, t_oth, start))
         table_term([(t_own, hid), (t_oth, oth)], GROUP, dwp, BF16)
+        table_2.wait_recv()
+        table_3.start()
         for c in by_side + leg_1:
             c.start()
         halve(1, [(s_oth, tab, whole)], False)
         send_other()
         table_term([(t_own, hid), (t_oth, oth)], 0, dwp, BF16)
-        table_2.wait_recv()
-        table_3.start()
 
     @pl.when(lo == 1)
     def _():
@@ -375,8 +389,6 @@
         table_last.wait_send()
         for i in range(3):
             grad_up[i].start()
-        leg_1[1].wait_recv()
-        leg_2[1].start()
 
     @pl.when(lo == 1)
     def _():
@@ -401,8 +413,7 @@
         table_up[7].wait_recv()
 
     slope(hid, arr, 0, base_arr, s_arr, t_arr, GROUP)
-    halve(0, [(s_arr, arr, second)], True)
-    send_own()
+    halve_own([(s_arr, arr, second)])
 
     @pl.when(lo == 1)
     def _():
@@ -415,6 +426,8 @@
 
     @pl.when(lo == 0)
     def _():
+        leg_1[1].wait_recv()
+        leg_2[1].start()
         grad_up[0].wait_send()
         grad_up[3].start()
         table_term([(t_arr, hid)], GROUP, grad, F32)
@@ -429,6 +442,7 @@
         grad[rows_of(cut)] = grad[rows_of(cut)] + dwr[rows_of(cut)].astype(F32)
 
     def finish_hidden():
+        core_copy(0, hi).wait_recv()
         for h in range(2):
             for late in range(2):
                 side_arrival(h, late).wait_recv()

time: 107 us -> 106 us (level)
  no operation moved by 1% of the time
where the time goes in v5:
time: 106 us
  Pallas kernels  102 us (96%)
  local copies, waits for them, and re-layouts  3.08 us (3%)
  between operations  1.29 us (1%)
    pallas_call x1, Pallas kernels, per_device(): pl.pallas_call(functools.partial(kernel, rows_of_ring), out_shape=(pltpu....  102 us
    unnamed x2, local copies, waits for them, and re-layouts  3.08 us

profile of v5, /device:TPU:1, one launch (start us, length us, event | category | flops | bytes accessed | tf_op | source)
XLA Modules:
  0.0 106.2 jit_solution(6771350789038658130)
XLA Ops:
  1.3 101.8 %shard_map.77 = (bf16[176,2304]{1,0:T(8,128)(2,1)S(1)}, f32[512,2304]{1,0:T(8,128)S(1)}) custom-call(s32[704]{0:T(1024)} %tgt_ref.1, s32[1]{0:T(128)S(6)} %copy.12.first_ref, f32[704]{0:T(1024)} %norm_ref.1, f32[704]{0:T(1024)} %cot_ref.1, bf16[704,2304]{1,0:T(8,128)(2,1)} %hid_hbm.1, bf16[512,2304]{1,0:T(8,128)(2,1)} %tab_hbm.1), custom_call_target="tpu_custom_call" | custom-call | flops 14948499456 | bytes 19464192 | tf_op jit(solution)/shard_map/pallas_call | solution.py:535
  103.1 0.9 copy.10
  104.0 2.2 %copy.11 = f32[512,2304]{1,0:T(8,128)} copy(f32[512,2304]{1,0:T(8,128)S(1)} %get-tuple-element.3) | data formatting | bytes 9437184

commit v6 on v5

--- a/solution.py
+++ b/solution.py
@@ -421,6 +421,7 @@
         halve(1, [(s_oth, arr, second)], True)
         send_other()
         hid_up[2].start()
+        hid_up[3].start()
         leg_2_odd[0].wait_recv()
         leg_3_odd[0].start()
 
@@ -461,12 +462,13 @@
             if i == 2:
                 leg_2[1].wait_recv()
                 leg_3[1].start()
+            if i == count - 1:
+                for n in range(2):
+                    leg_3[n].wait_recv()
+                    finish(LONG_CUTS[n])
+                finish_hidden()
             grad_up[i].wait_recv()
             finish(GRAD_CUTS[i])
-        for i in range(2):
-            leg_3[i].wait_recv()
-            finish(LONG_CUTS[i])
-        finish_hidden()
         for j, (h, low, size) in enumerate(SIDE_PARTS):
             by_back_in[j].wait_recv()
             finish((SIDE_CUTS[h][0] + low, size))
@@ -488,7 +490,6 @@
 
     @pl.when(lo == 1)
     def _():
-        hid_up[3].start()
         leg_2_odd[1].wait_recv()
         leg_3_odd[1].start()
         for j in range(2):

time: 106 us -> 106 us (level)
  no operation moved by 1% of the time
where the time goes in v6:
time: 106 us
  Pallas kernels  102 us (96%)
  local copies, waits for them, and re-layouts  3.08 us (3%)
  between operations  1.29 us (1%)
    pallas_call x1, Pallas kernels, per_device(): pl.pallas_call(functools.partial(kernel, rows_of_ring), out_shape=(pltpu....  102 us
    unnamed x2, local copies, waits for them, and re-layouts  3.08 us

profile of v6, /device:TPU:1, one launch (start us, length us, event | category | flops | bytes accessed | tf_op | source)
XLA Modules:
  0.0 106.2 jit_solution(13648438958049082358)
XLA Ops:
  1.3 101.8 %shard_map.77 = (bf16[176,2304]{1,0:T(8,128)(2,1)S(1)}, f32[512,2304]{1,0:T(8,128)S(1)}) custom-call(s32[704]{0:T(1024)} %tgt_ref.1, s32[1]{0:T(128)S(6)} %copy.12.first_ref, f32[704]{0:T(1024)} %norm_ref.1, f32[704]{0:T(1024)} %cot_ref.1, bf16[704,2304]{1,0:T(8,128)(2,1)} %hid_hbm.1, bf16[512,2304]{1,0:T(8,128)(2,1)} %tab_hbm.1), custom_call_target="tpu_custom_call" | custom-call | flops 14948499456 | bytes 19464192 | tf_op jit(solution)/shard_map/pallas_call | solution.py:536
  103.1 0.9 copy.10
  104.0 2.2 %copy.11 = f32[512,2304]{1,0:T(8,128)} copy(f32[512,2304]{1,0:T(8,128)S(1)} %get-tuple-element.3) | data formatting | bytes 9437184
